TPU v7x, 256 devices: a whole 4x4x8 slice. The times are simulated.
256 devices in a mesh: rx: 32 (over z, x_hi, core), tm: 8 (over y, x_lo).
Axes of the slice: x: 4 (x_hi: 2, x_lo: 2; x = x_hi * 2 + x_lo), y: 4, z: 8, core: 2. Of those that a mesh axis runs over, the one named last changes fastest.
Arguments:
- records: float32 [4096, 24576], P('rx', 'tm'), may hold values from -1000 to 1000, as said below
- source_block: int32 [2], replicated, may hold values from 0 to 63
- quality: int32 [4096], P('rx'), may hold values 0 or 1
Outputs:
- stacks: float32 [2, 64, 101, 4096], P(None, 'tm', None, 'rx')
Inputs may be any that keep to these rules, and one draw needn't show every extreme that they name: Noise records with channel and window gains.
All inputs are finite; a program needn't handle non-finite values. No bound on the sum of `quality` on one device may be relied on, other than what follows from the above.
Results may differ from a plain program's by a relative error of at most 0.0039.
Values may be sent and summed in bfloat16 or wider, within the bound.
A program may use at most 192 MiB of HBM per device.

v0:
```python
import math
import jax
import jax.numpy as jnp
from jax import lax
from jax.sharding import PartitionSpec as P

W = 1024
HALF = 50
LAGS = 101
SRC = 64
STEPS = 2


def broadcast(block, axis, owner):
    block = jnp.where(lax.axis_index(axis) == owner, block, jnp.zeros_like(block))
    return lax.psum(block, axis)


def whiten(records, quality):
    receivers = records.shape[0]
    samples = records.reshape(receivers, records.shape[1] // W, W)
    power = jnp.mean(samples * samples, axis=2, keepdims=True)
    return (samples * lax.rsqrt(power + 1e-06) * quality.astype(jnp.float32)[:, None, None]).astype(
        jnp.bfloat16
    )


def broadcast_block(whitened, block):
    per_device = whitened.shape[0]
    first_row = block * SRC
    owner = first_row // per_device
    offset = first_row - owner * per_device
    local_rows = lax.dynamic_slice_in_dim(whitened, offset, SRC, 0)
    return broadcast(local_rows, "rx", owner)


def lag_split():
    fine_shifts = math.isqrt(LAGS - 1) + 1
    coarse_shifts = -(-LAGS // fine_shifts)
    return (fine_shifts, coarse_shifts)


def source_stack(sources, fine_shifts):
    shifted = [
        jnp.pad(sources, ((0, 0), (0, 0), (offset, fine_shifts - offset)))
        for offset in range(fine_shifts)
    ]
    stacked = jnp.stack(shifted, 1)
    return stacked.reshape(sources.shape[0] * fine_shifts, -1)


def receiver_stack(whitened, fine_shifts, coarse_shifts):
    padded = jnp.pad(whitened, ((0, 0), (0, 0), (HALF, coarse_shifts * fine_shifts - HALF)))
    length = whitened.shape[2] + fine_shifts
    shifted = [
        padded[:, :, number * fine_shifts : number * fine_shifts + length]
        for number in range(coarse_shifts)
    ]
    stacked = jnp.stack(shifted, 1)
    return stacked.reshape(whitened.shape[0] * coarse_shifts, -1)


def lag_products(source_rows, receiver_rows, row_count, receivers, fine_shifts, coarse_shifts):
    products = lax.dot_general(
        source_rows, receiver_rows, (((1,), (1,)), ((), ())), preferred_element_type=jnp.float32
    )
    products = products.reshape(row_count, fine_shifts, receivers, coarse_shifts)
    products = jnp.transpose(products, (0, 3, 1, 2)).reshape(
        row_count, coarse_shifts * fine_shifts, receivers
    )
    return products[:, :LAGS, :]


def on_device(records, source_block, quality):
    receivers = records.shape[0]
    windows_here = records.shape[1] // W
    groups = lax.axis_size("tm")
    weight = 1.0 / math.sqrt(W * windows_here * groups)
    whitened = whiten(records, quality)
    fine_shifts, coarse_shifts = lag_split()
    sources = []
    for number in range(STEPS):
        sources.append(broadcast_block(whitened, source_block[number]))
    share_rows = SRC // groups
    receiver_rows = receiver_stack(whitened, fine_shifts, coarse_shifts)
    source_sets = [source_stack(block_rows, fine_shifts) for block_rows in sources]
    results = []
    for source_rows in source_sets:

        def step_term(first_row, row_count, source_rows=source_rows):
            return (
                lag_products(
                    source_rows, receiver_rows, row_count, receivers, fine_shifts, coarse_shifts
                )
                * weight
            )

        results.append(
            lax.psum_scatter(
                step_term(jnp.int32(0), share_rows * lax.axis_size("tm")),
                "tm",
                scatter_dimension=0,
                tiled=True,
            )
        )
    return jnp.stack(results, 0)


def solution(mesh):
    in_specs = (P("rx", "tm"), P(), P("rx"))
    out_specs = P(None, "tm", None, "rx")
    return jax.shard_map(
        on_device, mesh=mesh, in_specs=in_specs, out_specs=out_specs, check_vma=False
    )
```

profile of v0, /device:TPU:1, one launch (start us, length us, event | category | flops | bytes accessed | tf_op | source)
XLA Modules:
  0.0 485.6 jit_solution(4198167202444544092)
XLA Ops:
  6.5 1.3 fusion.16
  9.1 1.9 copy.7
  11.2 0.7 convert_element_type.41
  12.0 1.7 dynamic-slice_select_fusion.1
  13.8 1.2 bitcast_dynamic-update-slice_fusion.20
  15.0 1.1 bitcast_dynamic-update-slice_fusion.19
  16.1 1.1 bitcast_dynamic-update-slice_fusion.18
  17.2 1.1 bitcast_dynamic-update-slice_fusion.17
  18.2 1.1 bitcast_dynamic-update-slice_fusion.16
  19.3 1.2 bitcast_dynamic-update-slice_fusion.15
  20.5 1.0 bitcast_dynamic-update-slice_fusion.14
  21.5 1.1 bitcast_dynamic-update-slice_fusion.13
  22.5 1.1 bitcast_dynamic-update-slice_fusion.12
  23.7 1.1 bitcast_dynamic-update-slice_fusion.11
  24.7 266.0 %all-reduce.26.cloned.1.call-done = (bf16[64,3,1024]{0,2,1:T(8,128)(2,1)}, bf16[64,3,1024]{0,2,1:T(8,128)(2,1)}) async-done(((bf16[64,3,1024]{0,2,1:T(8,128)(2,1)}, bf16[64,3,1024]{0,2,1:T(8,128)(2,1)}), (bf16[64,3,1024]{0,2,1:T(8,128)(2,1)}, bf16[64,3,1024]{0,2,1:T(8,128)(2,1)})) %all-reduce.26.cloned.1.call-update) | async-done | bytes 786448 | tf_op jit(solution)/shard_map/psum | solution.py:16
  290.7 1.4 bitcast_dynamic-update-slice_fusion.31
  292.1 1.4 bitcast_dynamic-update-slice_fusion.30
  293.6 1.4 bitcast_dynamic-update-slice_fusion.29
  295.0 1.4 bitcast_dynamic-update-slice_fusion.28
  296.5 1.4 bitcast_dynamic-update-slice_fusion.27
  297.9 1.4 bitcast_dynamic-update-slice_fusion.26
  299.3 0.3 bitcast_dynamic-update-slice_fusion.25
  300.2 0.3 bitcast_dynamic-update-slice_fusion.22
  303.3 0.6 bitcast_dynamic-update-slice_fusion
  303.9 3.4 copy-done.2
  307.3 10.3 %fusion.6 = f32[64,10,11,128]{3,0,1,2:T(8,128)S(1)} fusion(bf16[128,10,3,1035]{0,3,2,1:T(8,128)(2,1)} %bitcast_dynamic-update-slice_fusion.11, bf16[64,11,3,1035]{0,3,2,1:T(8,128)(2,1)S(1)} %get-tuple-element.12), kind=kOutput, calls=%fused_computation.8 | convolution fusion | flops 5595955200 | bytes 15925120 | tf_op jit(solution)/shard_map/dot_general | solution.py:64
  317.9 2.1 slice_multiply_fusion.1
  320.1 12.5 %fusion.11 = f32[64,10,11,128]{3,0,1,2:T(8,128)S(1)} fusion(bf16[128,10,3,1035]{0,3,2,1:T(8,128)(2,1)} %bitcast_dynamic-update-slice_fusion.11, bf16[64,11,3,1035]{0,3,2,1:T(8,128)(2,1)} %copy-done.2), kind=kOutput, calls=%fused_computation.9 | convolution fusion | flops 5595955200 | bytes 15925120 | tf_op jit(solution)/shard_map/dot_general | solution.py:64
  332.9 2.1 slice_multiply_fusion
  335.0 61.6 %reduce-scatter.3.cloned.1.call-done = f32[8,101,128]{2,0,1:T(8,128)} async-done(((f32[64,101,128]{2,0,1:T(8,128)}), f32[8,101,128]{2,0,1:T(8,128)}) %reduce-scatter.3.cloned.1.call-update) | async-done | bytes 413712 | tf_op jit(solution)/shard_map/reduce_scatter | solution.py:99
  396.5 80.4 %reduce-scatter.5.cloned.1.call-done = f32[8,101,128]{2,0,1:T(8,128)} async-done(((f32[64,101,128]{2,0,1:T(8,128)}), f32[8,101,128]{2,0,1:T(8,128)}) %reduce-scatter.5.cloned.1.call-update) | async-done | bytes 413712 | tf_op jit(solution)/shard_map/reduce_scatter | solution.py:99
  477.0 2.1 pad_maximum_fusion
  (28 shorter events, 4.3 us)
Async XLA Ops:
  6.5 284.2 %all-reduce.26.cloned.1.call-start = ((), (), s32[]{:S(2)}) async-start(), calls=%async_computation.4 | async-start | bytes 3145728 | tf_op jit(solution)/shard_map/psum | solution.py:16
  13.7 382.8 %reduce-scatter.3.cloned.1.call-start = ((), (), s32[]{:S(2)}) async-start(), calls=%async_computation.2 | async-start | bytes 3723264 | tf_op jit(solution)/shard_map/reduce_scatter | solution.py:99
  290.7 8.6 %copy-start.1 = (bf16[64,3,1024]{0,2,1:T(8,128)(2,1)S(1)}, bf16[64,3,1024]{0,2,1:T(8,128)(2,1)}, u32[]{:S(2)}) copy-start(bf16[64,3,1024]{0,2,1:T(8,128)(2,1)} %get-tuple-element.6) | copy-start | bytes 1179652
  290.7 9.7 %copy-start = (bf16[64,3,1024]{0,2,1:T(8,128)(2,1)S(1)}, bf16[64,3,1024]{0,2,1:T(8,128)(2,1)}, u32[]{:S(2)}) copy-start(bf16[64,3,1024]{0,2,1:T(8,128)(2,1)} %get-tuple-element.5) | copy-start | bytes 1179652
  303.9 3.4 copy-start.2
  320.0 156.9 %reduce-scatter.5.cloned.1.call-start = ((), (), s32[]{:S(2)}) async-start(), calls=%async_computation.3 | async-start | bytes 3723264 | tf_op jit(solution)/shard_map/reduce_scatter | solution.py:99
Sparse Core Ops, SparseCore 0:
  13.9 276.8 all-reduce.25
  320.1 76.3 reduce-scatter.2
  399.3 77.6 reduce-scatter.4
where the time goes:
time: 486 us
  waiting for transfers between devices  408 us (84%)
  local copies, waits for them, and re-layouts  31.1 us (6%)
  matrix products  22.9 us (5%)
  between operations  14.5 us (3%)
  other arithmetic  8.97 us (2%)
    psum x1, waiting for transfers between devices, broadcast(): return lax.psum(block, axis)  266 us
    reduce_scatter x2, waiting for transfers between devices, on_device(): lax.psum_scatter(step_term(jnp.int32(0), share_rows * lax.axis_size('tm')...  142 us
    unnamed x36, local copies, waits for them, and re-layouts  27.6 us
    dot_general x2, matrix products, lag_products(): lax.dot_general(source_rows, receiver_rows, (((1,), (1,)), ((), ())), pre...  22.9 us
  transfers between devices with their start and end apart: 3, of which 3 were waited for; matrix products, arithmetic and copies ran while one was open for 5% of the time, Pallas kernels for 0%

commit v1 on v0

--- a/solution.py
+++ b/solution.py
@@ -13,7 +13,7 @@
 
 def broadcast(block, axis, owner):
     block = jnp.where(lax.axis_index(axis) == owner, block, jnp.zeros_like(block))
-    return lax.psum(block, axis)
+    return jnp.sum(lax.all_gather(block, axis), axis=0)
 
 
 def whiten(records, quality):

time: 486 us -> 419 us (0.86)
  waiting for transfers between devices: 408 us -> 340 us
  other arithmetic: 8.97 us -> 23.1 us
  local copies, waits for them, and re-layouts: 31.1 us -> 20.9 us
    psum x1 -> x0, waiting for transfers between devices: 266 us -> none  [broadcast(): return lax.psum(block, axis)]
    all_gather x0 -> x2, waiting for transfers between devices: none -> 205 us  [broadcast(): return jnp.sum(lax.all_gather(block, axis), axis=0)]
    reduce_sum x0 -> x2, other arithmetic: none -> 15.3 us  [broadcast(): return jnp.sum(lax.all_gather(block, axis), axis=0)]
    unnamed x36 -> x30, local copies, waits for them, and re-layouts: 27.6 us -> 15.3 us
    reduce_scatter x2, waiting for transfers between devices: 142 us -> 135 us  [on_device(): lax.psum_scatter(step_term(jnp.int32(0), share_rows * lax.axis_size('tm')...]
  transfers between devices with their start and end apart: 3 -> 4, of which waited for: 3 -> 4; matrix products, arithmetic and copies ran while one was open for 5% -> 13% of each run, Pallas kernels for 0% -> 0%
where the time goes in v1:
time: 419 us; the launch traced here: 418 us
  waiting for transfers between devices  340 us (81%)
  other arithmetic  23.1 us (6%)
  local copies, waits for them, and re-layouts  20.9 us (5%)
  matrix products  19.7 us (5%)
  between operations  14.7 us (4%)
    all_gather x2, waiting for transfers between devices, broadcast(): return jnp.sum(lax.all_gather(block, axis), axis=0)  205 us
    reduce_scatter x2, waiting for transfers between devices, on_device(): lax.psum_scatter(step_term(jnp.int32(0), share_rows * lax.axis_size('tm')...  135 us
    dot_general x2, matrix products, lag_products(): lax.dot_general(source_rows, receiver_rows, (((1,), (1,)), ((), ())), pre...  19.7 us
    unnamed x30, local copies, waits for them, and re-layouts  15.3 us
    reduce_sum x2, other arithmetic, broadcast(): return jnp.sum(lax.all_gather(block, axis), axis=0)  15.3 us
  transfers between devices with their start and end apart: 4, of which 4 were waited for; matrix products, arithmetic and copies ran while one was open for 13% of the time, Pallas kernels for 0%

profile of v1, /device:TPU:1, one launch (start us, length us, event | category | flops | bytes accessed | tf_op | source)
XLA Modules:
  0.0 418.4 jit_solution(12007948197085296933)
XLA Ops:
  6.5 1.4 fusion.16
  9.3 1.9 copy.10
  11.2 0.7 convert_element_type.45
  12.2 0.6 dynamic-slice_select_fusion.1
  12.8 1.0 copy.13
  13.9 1.0 copy.11
  15.0 1.1 bitcast_dynamic-update-slice_fusion.9
  16.1 1.1 bitcast_dynamic-update-slice_fusion.8
  17.2 1.1 bitcast_dynamic-update-slice_fusion.7
  18.3 1.1 bitcast_dynamic-update-slice_fusion.6
  19.4 1.1 bitcast_dynamic-update-slice_fusion.5
  20.5 1.1 bitcast_dynamic-update-slice_fusion.4
  21.6 1.0 bitcast_dynamic-update-slice_fusion.3
  22.6 1.1 bitcast_dynamic-update-slice_fusion.2
  23.7 1.1 bitcast_dynamic-update-slice_fusion.1
  24.8 1.1 bitcast_dynamic-update-slice_fusion
  25.9 109.6 %all-gather.7.cloned.1.call-done = bf16[2048,3,1024]{2,0,1:T(8,128)(2,1)} async-done(((bf16[64,3,1024]{2,0,1:T(8,128)(2,1)}), bf16[2048,3,1024]{2,0,1:T(8,128)(2,1)}) %all-gather.7.cloned.1.call-update) | async-done | bytes 12582928 | tf_op jit(solution)/shard_map/all_gather | solution.py:16
  135.5 7.6 %reduce_sum.35 = bf16[64,3,1024]{2,0,1:T(8,128)(2,1)S(1)} reduce(bf16[32,64,3,1024]{3,1,0,2:T(8,128)(2,1)} %bitcast.111, bf16[]{:T(256)} %constant.47.clone.1), dimensions={0}, to_apply=%region_3.4 | reduce | flops 6094848 | bytes 12976130 | tf_op jit(solution)/shard_map/reduce_sum | solution.py:16
  143.2 0.2 bitcast_dynamic-update-slice_fusion.19
  143.8 0.2 bitcast_dynamic-update-slice_fusion.16
  144.2 0.2 bitcast_dynamic-update-slice_fusion.14
  145.2 9.8 %fusion.11 = f32[64,10,11,128]{3,0,1,2:T(8,128)S(1)} fusion(bf16[128,10,3,1035]{0,3,2,1:T(8,128)(2,1)} %bitcast_dynamic-update-slice_fusion, bf16[64,11,3,1035]{3,0,2,1:T(8,128)(2,1)S(1)} %bitcast_dynamic-update-slice_fusion.10), kind=kOutput, calls=%fused_computation.9 | convolution fusion | flops 5595955200 | bytes 15925120 | tf_op jit(solution)/shard_map/dot_general | solution.py:64
  155.0 0.4 copy.14
  155.5 2.1 slice_multiply_fusion
  157.6 95.2 %all-gather.5.cloned.1.call-done = bf16[2048,3,1024]{2,0,1:T(8,128)(2,1)} async-done(((bf16[64,3,1024]{2,0,1:T(8,128)(2,1)}), bf16[2048,3,1024]{2,0,1:T(8,128)(2,1)}) %all-gather.5.cloned.1.call-update) | async-done | bytes 12582928 | tf_op jit(solution)/shard_map/all_gather | solution.py:16
  252.8 7.6 %reduce_sum.34 = bf16[64,3,1024]{2,0,1:T(8,128)(2,1)S(1)} reduce(bf16[32,64,3,1024]{3,1,0,2:T(8,128)(2,1)} %bitcast.110, bf16[]{:T(256)} %constant.47.clone.1), dimensions={0}, to_apply=%region_1.2 | reduce | flops 6094848 | bytes 12976130 | tf_op jit(solution)/shard_map/reduce_sum | solution.py:16
  262.5 9.9 %fusion.6 = f32[64,10,11,128]{3,0,1,2:T(8,128)S(1)} fusion(bf16[128,10,3,1035]{0,3,2,1:T(8,128)(2,1)} %bitcast_dynamic-update-slice_fusion, bf16[64,11,3,1035]{3,0,2,1:T(8,128)(2,1)S(1)} %bitcast_dynamic-update-slice_fusion.21), kind=kOutput, calls=%fused_computation.8 | convolution fusion | flops 5595955200 | bytes 15925120 | tf_op jit(solution)/shard_map/dot_general | solution.py:64
  272.3 0.3 copy.12
  272.6 2.1 slice_multiply_fusion.1
  274.7 55.0 %reduce-scatter.5.cloned.1.call-done = f32[8,101,128]{2,0,1:T(8,128)} async-done(((f32[64,101,128]{2,0,1:T(8,128)}), f32[8,101,128]{2,0,1:T(8,128)}) %reduce-scatter.5.cloned.1.call-update) | async-done | bytes 413712 | tf_op jit(solution)/shard_map/reduce_scatter | solution.py:99
  329.7 80.1 %reduce-scatter.3.cloned.1.call-done = f32[8,101,128]{2,0,1:T(8,128)} async-done(((f32[64,101,128]{2,0,1:T(8,128)}), f32[8,101,128]{2,0,1:T(8,128)}) %reduce-scatter.3.cloned.1.call-update) | async-done | bytes 413712 | tf_op jit(solution)/shard_map/reduce_scatter | solution.py:99
  409.8 2.1 pad_maximum_fusion
  (30 shorter events, 4.0 us)
Async XLA Ops:
  6.5 129.0 %all-gather.7.cloned.1.call-start = ((), (), s32[]{:S(2)}) async-start(), calls=%async_computation.5 | async-start | bytes 12976128 | tf_op jit(solution)/shard_map/all_gather | solution.py:16
  13.8 238.9 %all-gather.5.cloned.1.call-start = ((), (), s32[]{:S(2)}) async-start(), calls=%async_computation.4 | async-start | bytes 12976128 | tf_op jit(solution)/shard_map/all_gather | solution.py:16
  14.9 314.8 %reduce-scatter.5.cloned.1.call-start = ((), (), s32[]{:S(2)}) async-start(), calls=%async_computation.3 | async-start | bytes 3723264 | tf_op jit(solution)/shard_map/reduce_scatter | solution.py:99
  157.6 252.2 %reduce-scatter.3.cloned.1.call-start = ((), (), s32[]{:S(2)}) async-start(), calls=%async_computation.2 | async-start | bytes 3723264 | tf_op jit(solution)/shard_map/reduce_scatter | solution.py:99
Sparse Core Ops, SparseCore 0:
  14.0 121.4 all-gather.6
  138.3 114.4 all-gather.4
  255.4 74.2 reduce-scatter.4
  332.1 77.6 reduce-scatter.2
